TPU v7x, 32 devices: a whole 2x2x4 slice. The times are simulated.
32 devices in a mesh: wide: 8 (over z, x), narrow: 4 (over y, core).
Axes of the slice: x: 2, y: 2, z: 4, core: 2. Of those that a mesh axis runs over, the one named last changes fastest.
Arguments:
- tokens: bfloat16 [49152, 512], P(('wide', 'narrow')), may hold values from -6 to 6
- window_lengths: int32 [32, 6], P(('wide', 'narrow')), may hold values from 0 to 1024, as said below
- conv_weight: bfloat16 [9, 512, 512], P(None, 'wide', 'narrow'), may hold values from -0.09375 to 0.09375
- feedforward_input_weight: bfloat16 [512, 2048], P('wide', 'narrow'), may hold values from -0.25 to 0.25
- ffn_out: bfloat16 [2048, 512], P('wide', 'narrow'), may hold values from -0.125 to 0.125
- small_params: bfloat16 [5120], P(('wide', 'narrow')), may hold values from -1.25 to 1.625
- cotangent: bfloat16 [49152, 512], P(('wide', 'narrow')), may hold values from -6 to 6
Outputs:
- block_out: bfloat16 [49152, 512], P(('wide', 'narrow'))
- grad_tokens: float32 [49152, 512], P(('wide', 'narrow'))
- convolution_weight_gradient: float32 [9, 512, 512], P(None, 'wide', 'narrow')
- grad_ffn_in: float32 [512, 2048], P('wide', 'narrow')
- grad_ffn_out: float32 [2048, 512], P('wide', 'narrow')
- grad_small: float32 [5120], P(('wide', 'narrow'))
Inputs may be any that keep to these rules, and one draw needn't show every extreme that they name: `window_lengths`: each row lists its device's window lengths in order, each 256, 512 or 1024, then zeros; the first is 1024 and their sum is at most 1536.
All inputs are finite; a program needn't handle non-finite values.
Results may differ from a plain program's by a relative error of at most 0.0064.
Values may be sent and summed in bfloat16 or wider, within the bound.
A program may use at most 192 MiB of HBM per device.

v0:
```python
import jax
import jax.numpy as jnp
from jax import lax
from jax.sharding import PartitionSpec as P

D = 512
FF = 2048
KERNEL_TAPS = 9
DILATION_STEP = 8


EPSILON = 1e-05


def layer_norm(values, norm_gain, norm_shift):
    centre = values - jnp.mean(values, axis=-1, keepdims=True)
    spread = jnp.mean(centre * centre, axis=-1, keepdims=True)
    return centre * lax.rsqrt(spread + EPSILON) * norm_gain + norm_shift


def window_masks(lengths, row_count):
    bounds = jnp.cumsum(lengths)
    places = jnp.arange(row_count, dtype=jnp.int32)
    segment_ids = jnp.sum((places[:, None] >= bounds[None, :]).astype(jnp.int32), axis=1)
    live_rows = (places < bounds[-1]).astype(jnp.float32)
    tap_valid = []
    for index_of_tap in range(KERNEL_TAPS):
        tap_displacement = (index_of_tap - KERNEL_TAPS // 2) * DILATION_STEP
        source = places + tap_displacement
        inside = (source >= 0) & (source < row_count)
        same_window = jnp.roll(segment_ids, -tap_displacement) == segment_ids
        tap_valid.append((inside & same_window).astype(jnp.float32))
    return (live_rows, tap_valid)


def split_params(flat_params):
    return (
        flat_params[0:D],
        flat_params[D : 2 * D],
        flat_params[2 * D : 3 * D],
        flat_params[3 * D : 3 * D + FF],
        flat_params[3 * D + FF : 4 * D + FF],
        flat_params[4 * D + FF : 5 * D + FF],
        flat_params[5 * D + FF : 6 * D + FF],
    )


def branch_one(conv_sum, conv_bias, gain_one, shift_one):
    return layer_norm(jax.nn.gelu(conv_sum + conv_bias), gain_one, shift_one)


def branch_two(outer_sum, outer_bias, gain_two, shift_two):
    return layer_norm(outer_sum + outer_bias, gain_two, shift_two)


def fetch_forward(conv_weight, feedforward_input_weight, ffn_out, small_params):
    narrow_set = (
        lax.all_gather(conv_weight, "narrow", axis=2, tiled=True),
        lax.all_gather(feedforward_input_weight, "narrow", axis=1, tiled=True),
        lax.all_gather(ffn_out, "narrow", axis=1, tiled=True),
        lax.all_gather(small_params, "narrow", axis=0, tiled=True),
    )
    return (
        lax.all_gather(narrow_set[0], "wide", axis=1, tiled=True),
        lax.all_gather(narrow_set[1], "wide", axis=0, tiled=True),
        lax.all_gather(narrow_set[2], "wide", axis=0, tiled=True),
        lax.all_gather(narrow_set[3], "wide", axis=0, tiled=True),
    )


def fetch_backward(conv_weight, feedforward_input_weight, ffn_out, small_params):
    narrow_set = (
        lax.all_gather(conv_weight, "narrow", axis=2, tiled=True),
        lax.all_gather(feedforward_input_weight, "narrow", axis=1, tiled=True),
        lax.all_gather(ffn_out, "narrow", axis=1, tiled=True),
        lax.all_gather(small_params, "narrow", axis=0, tiled=True),
    )
    return (
        lax.all_gather(narrow_set[0], "wide", axis=1, tiled=True),
        lax.all_gather(narrow_set[1], "wide", axis=0, tiled=True),
        lax.all_gather(narrow_set[2], "wide", axis=0, tiled=True),
        lax.all_gather(narrow_set[3], "wide", axis=0, tiled=True),
    )


def shards(
    tokens, window_lengths, conv_weight, feedforward_input_weight, ffn_out, small_params, cotangent
):
    row_count = tokens.shape[0]
    block_size = min(512, row_count)
    live_rows, tap_valid = window_masks(window_lengths[0], row_count)
    weights = fetch_forward(conv_weight, feedforward_input_weight, ffn_out, small_params)
    conv_full, inner_full, outer_full = (weights[0], weights[1], weights[2])
    pieces = split_params(weights[3].astype(jnp.float32))
    start_rows = tokens * live_rows[:, None].astype(jnp.bfloat16)
    conv_sum = jnp.zeros((row_count, D), jnp.float32)
    for index_of_tap in range(KERNEL_TAPS):
        tap_displacement = (index_of_tap - KERNEL_TAPS // 2) * DILATION_STEP
        shifted = jnp.roll(start_rows, -tap_displacement, axis=0) * tap_valid[index_of_tap][
            :, None
        ].astype(jnp.bfloat16)
        conv_sum = conv_sum + jnp.dot(
            shifted, conv_full[index_of_tap], preferred_element_type=jnp.float32
        )
    branch_out, pull_one = jax.vjp(branch_one, conv_sum, pieces[0], pieces[1], pieces[2])
    residual_one = start_rows.astype(jnp.float32) + branch_out
    residual_low = residual_one.astype(jnp.bfloat16)
    outer_parts = []
    for first_row in range(0, row_count, block_size):
        inner_sum = (
            jnp.dot(
                residual_low[first_row : first_row + block_size],
                inner_full,
                preferred_element_type=jnp.float32,
            )
            + pieces[3]
        )
        active = jax.nn.gelu(inner_sum).astype(jnp.bfloat16)
        outer_parts.append(jnp.dot(active, outer_full, preferred_element_type=jnp.float32))
    outer_sum = jnp.concatenate(outer_parts, axis=0)
    normed, pull_two = jax.vjp(branch_two, outer_sum, pieces[4], pieces[5], pieces[6])
    block_out = (live_rows[:, None] * (residual_one + normed)).astype(jnp.bfloat16)
    upstream = cotangent.astype(jnp.float32) * live_rows[:, None]
    d_outer, d_outer_bias, d_gain_two, d_shift_two = pull_two(upstream)
    outer_low = d_outer.astype(jnp.bfloat16)
    weights = fetch_backward(conv_weight, feedforward_input_weight, ffn_out, small_params)
    conv_full, inner_full, outer_full = (weights[0], weights[1], weights[2])
    pieces = split_params(weights[3].astype(jnp.float32))
    grad_in = jnp.zeros((D, FF), jnp.float32)
    grad_out = jnp.zeros((FF, D), jnp.float32)
    inner_bias_grad = jnp.zeros((FF,), jnp.float32)
    resid_parts = []
    for first_row in range(0, row_count, block_size):
        rows_low = residual_low[first_row : first_row + block_size]
        outer_rows = outer_low[first_row : first_row + block_size]
        inner_sum = jnp.dot(rows_low, inner_full, preferred_element_type=jnp.float32) + pieces[3]
        active_full, pull_gelu = jax.vjp(jax.nn.gelu, inner_sum)
        active = active_full.astype(jnp.bfloat16)
        d_active = jnp.einsum(
            "rd,fd->rf", outer_rows, outer_full, preferred_element_type=jnp.float32
        )
        d_inner = pull_gelu(d_active)[0]
        inner_bias_grad = inner_bias_grad + jnp.sum(d_inner, axis=0)
        inner_low = d_inner.astype(jnp.bfloat16)
        grad_in = grad_in + jnp.einsum(
            "rd,rf->df", rows_low, inner_low, preferred_element_type=jnp.float32
        )
        grad_out = grad_out + jnp.einsum(
            "rf,rd->fd", active, outer_rows, preferred_element_type=jnp.float32
        )
        resid_parts.append(
            jnp.einsum("rf,df->rd", inner_low, inner_full, preferred_element_type=jnp.float32)
        )
    d_resid = upstream + jnp.concatenate(resid_parts, axis=0)
    d_conv, d_conv_bias, d_gain_one, d_shift_one = pull_one(d_resid)
    convolution_reduced = d_conv.astype(jnp.bfloat16)
    conv_grads = []
    d_start = d_resid
    for index_of_tap in range(KERNEL_TAPS):
        tap_displacement = (index_of_tap - KERNEL_TAPS // 2) * DILATION_STEP
        tap_mask = tap_valid[index_of_tap][:, None]
        shifted = jnp.roll(start_rows, -tap_displacement, axis=0) * tap_mask.astype(jnp.bfloat16)
        conv_grads.append(
            jnp.einsum(
                "ri,ro->io", shifted, convolution_reduced, preferred_element_type=jnp.float32
            )
        )
        back_rows = jnp.einsum(
            "ro,io->ri",
            convolution_reduced,
            conv_full[index_of_tap],
            preferred_element_type=jnp.float32,
        )
        d_start = d_start + jnp.roll(back_rows * tap_mask, tap_displacement, axis=0)
    grad_tokens = d_start * live_rows[:, None]
    convolution_weight_gradient = jnp.stack(conv_grads, axis=0)
    grad_flat = jnp.concatenate(
        [
            d_conv_bias,
            d_gain_one,
            d_shift_one,
            inner_bias_grad,
            d_outer_bias,
            d_gain_two,
            d_shift_two,
        ],
        axis=0,
    )
    wide_sums = (
        lax.psum_scatter(convolution_weight_gradient, "wide", scatter_dimension=1, tiled=True),
        lax.psum_scatter(grad_in, "wide", scatter_dimension=0, tiled=True),
        lax.psum_scatter(grad_out, "wide", scatter_dimension=0, tiled=True),
        lax.psum_scatter(grad_flat, "wide", scatter_dimension=0, tiled=True),
    )
    owned = (
        lax.psum_scatter(wide_sums[0], "narrow", scatter_dimension=2, tiled=True),
        lax.psum_scatter(wide_sums[1], "narrow", scatter_dimension=1, tiled=True),
        lax.psum_scatter(wide_sums[2], "narrow", scatter_dimension=1, tiled=True),
        lax.psum_scatter(wide_sums[3], "narrow", scatter_dimension=0, tiled=True),
    )
    owned_flat = owned[3]
    return (block_out, grad_tokens, owned[0], owned[1], owned[2], owned_flat)


def solution(mesh):
    return jax.shard_map(
        shards,
        mesh=mesh,
        in_specs=(
            P(("wide", "narrow"), None),
            P(("wide", "narrow"), None),
            P(None, "wide", "narrow"),
            P("wide", "narrow"),
            P("wide", "narrow"),
            P(("wide", "narrow")),
            P(("wide", "narrow"), None),
        ),
        out_specs=(
            P(("wide", "narrow"), None),
            P(("wide", "narrow"), None),
            P(None, "wide", "narrow"),
            P("wide", "narrow"),
            P("wide", "narrow"),
            P(("wide", "narrow")),
        ),
        check_vma=False,
    )
```

profile of v0, /device:TPU:0, one launch (start us, length us, event | category | flops | bytes accessed | tf_op | source)
XLA Modules:
  0.0 649.9 jit_solution(4908927474395452969)
XLA Ops:
  7.2 10.7 %all_gather.32 = bf16[9,64,512]{2,1,0:T(8,128)(2,1)} all-gather(bf16[9,64,128]{2,1,0:T(8,128)(2,1)} %param.9), channel_id=1, replica_groups=mesh['wide'=8,'narrow'=4] {'narrow'}, dimensions={2}, use_global_device_ids=true | all-gather | bytes 737280 | tf_op jit(solution)/shard_map/all_gather | solution.py:58
  18.0 6.6 %all_gather.36 = bf16[64,2048]{1,0:T(8,128)(2,1)} all-gather(bf16[64,512]{1,0:T(8,128)(2,1)} %param.10), channel_id=1, replica_groups=mesh['wide'=8,'narrow'=4] {'narrow'}, dimensions={1}, use_global_device_ids=true | all-gather | bytes 327680 | tf_op jit(solution)/shard_map/all_gather | solution.py:59
  24.7 8.0 %all_gather.38 = bf16[256,512]{1,0:T(8,128)(2,1)} all-gather(bf16[256,128]{1,0:T(8,128)(2,1)} %param.11), channel_id=1, replica_groups=mesh['wide'=8,'narrow'=4] {'narrow'}, dimensions={1}, use_global_device_ids=true | all-gather | bytes 327680 | tf_op jit(solution)/shard_map/all_gather | solution.py:60
  57.4 6.4 all-reduce
  63.8 31.2 %all-gather = bf16[8,1,640]{2,1,0:T(2,128)(2,1)S(1)} all-gather(bf16[1,1,640]{2,1,0:T(2,128)(2,1)S(1)} %reshape.436), channel_id=1, replica_groups=mesh['wide'=8,'narrow'=4] {'wide'}, dimensions={0}, use_global_device_ids=true | all-gather | bytes 11520 | tf_op jit(solution)/shard_map/all_gather | solution.py:67
  118.5 3.0 fusion.155
  121.5 26.8 %all-gather.7.cloned.1.call-done = bf16[512,2048]{1,0:T(8,128)(2,1)} async-done(((bf16[64,2048]{1,0:T(8,128)(2,1)}), bf16[512,2048]{1,0:T(8,128)(2,1)}) %all-gather.7.cloned.1.call-update) | async-done | bytes 2097168 | tf_op jit(solution)/shard_map/all_gather | solution.py:65
  148.3 3.2 fusion.88
  155.5 6.4 multiply_convert_fusion.2
  161.9 36.4 %all-gather.9.cloned.1.call-done = bf16[2048,512]{1,0:T(8,128)(2,1)} async-done(((bf16[256,512]{1,0:T(8,128)(2,1)}), bf16[2048,512]{1,0:T(8,128)(2,1)}) %all-gather.9.cloned.1.call-update) | async-done | bytes 2097168 | tf_op jit(solution)/shard_map/all_gather | solution.py:66
  198.3 3.7 fusion.200
  216.1 3.3 add_add_fusion.2
  219.5 7.5 %fusion.198 = (f32[2048]{0:T(1024)}, bf16[512,2048]{1,0:T(8,128)(2,1)S(1)}) fusion(f32[512,2048]{1,0:T(8,128)} %get-tuple-element.115, f32[2048]{0:T(1024)} %slice.407, bf16[2048,512]{1,0:T(8,128)(2,1)} %all-gather.9.cloned.1.call-done, bf16[1536,512]{0,1:T(8,128)(2,1)} %copy-done.38), kind=kOutput, calls=%fused_computation.287 | convolution fusion | flops 1096808448 | bytes 8929280 | tf_op jit(solution)/shard_map/rd,fd->rf/dot_general | solution.py:139
  230.4 4.8 fusion.199
  238.2 4.6 fusion.197
  244.2 3.3 add_add_fusion.3
  247.6 3.7 fusion.62
  254.8 3.0 fusion.160
  261.5 7.2 %fusion.161 = (f32[512]{0:T(512)}, bf16[1536,512]{0,1:T(8,128)(2,1)S(1)}, bf16[1536,512]{0,1:T(8,128)(2,1)}) fusion(f32[1536,512]{0,1:T(8,128)S(1)} %copy-done.1, f32[1536]{0:T(1024)S(1)} %negate_multiply_fusion, f32[1536]{0:T(1024)S(1)} %multiply_multiply_fusion.9, f32[1536]{0:T(1024)S(1)} %broadcast_multiply_fusion.2, f32[1536]{0:T(1024)S(1)} %copy-done.65, ...), kind=kLoop, calls=%fused_computation.259 | loop fusion | flops 35388928 | bytes 14214144 | tf_op jit(solution)/shard_map/transpose(jvp())/reduce_sum | solution.py:49
  289.7 16.2 %reduce-scatter.15.cloned.1.call-done = f32[256,512]{1,0:T(8,128)} async-done(((f32[2048,512]{1,0:T(8,128)}), f32[256,512]{1,0:T(8,128)}) %reduce-scatter.15.cloned.1.call-update) | async-done | bytes 524304 | tf_op jit(solution)/shard_map/reduce_scatter | solution.py:192
  306.0 3.7 convolution_multiply_fusion.8
  309.7 3.7 convolution_multiply_fusion.7
  313.4 3.8 convolution_multiply_fusion.6
  317.3 80.3 %reduce-scatter.11.cloned.1.call-done = f32[64,2048]{1,0:T(8,128)} async-done(((f32[512,2048]{1,0:T(8,128)}), f32[64,2048]{1,0:T(8,128)}) %reduce-scatter.11.cloned.1.call-update) | async-done | bytes 524304 | tf_op jit(solution)/shard_map/reduce_scatter | solution.py:191
  397.9 3.7 convolution_multiply_fusion.5
  401.6 3.7 convolution_multiply_fusion.3
  405.2 3.7 convolution_multiply_fusion.2
  409.0 155.6 %reduce-scatter.7.cloned.1.call-done = f32[9,64,512]{2,1,0:T(8,128)} async-done(((f32[9,512,512]{2,1,0:T(8,128)}), f32[9,64,512]{2,1,0:T(8,128)}) %reduce-scatter.7.cloned.1.call-update) | async-done | bytes 1179664 | tf_op jit(solution)/shard_map/reduce_scatter | solution.py:190
  582.9 12.5 %fusion.24 = f32[1536,512]{0,1:T(8,128)} fusion(bf16[1536,512]{0,1:T(8,128)(2,1)S(1)} %get-tuple-element.34, f32[1536,512]{0,1:T(8,128)S(1)} %copy-done.3, f32[32,512]{0,1:T(8,128)S(1)} %slice-done.2, f32[1504,512]{0,1:T(8,128)} %slice.416, f32[24,512]{0,1:T(8,128)S(1)} %slice-done.1, f32[1512,512]{0,1:T(8,128)} %slice.418, f32[16,512]{0,1:T(8,128)S(1)} %slice-done, ...), kind=kOutput, calls=%fused_computation.56 | convolution fusion | flops 820248576 | bytes 33779712 | tf_op jit(solution)/shard_map/ro,io->ri/dot_general | solution.py:168
  595.4 3.7 copy.69
  600.9 35.2 %all-reduce.1 = f32[5120]{0:T(1024)S(1)} all-reduce(f32[5120]{0:T(1024)S(1)} %constant_dynamic-update-slice_fusion.1), channel_id=8, replica_groups=mesh['wide'=8,'narrow'=4] {'wide'}, use_global_device_ids=true, to_apply=%region_25.26.clone | all-reduce | flops 5120 | bytes 40960
  636.2 6.1 all-reduce.2
  (380 shorter events, 120.6 us)
Async XLA Ops:
  7.2 33.0 %copy-start.52 = (bf16[1536,512]{1,0:T(8,128)(2,1)S(1)}, bf16[1536,512]{1,0:T(8,128)(2,1)}, u32[]{:S(2)}) copy-start(bf16[1536,512]{1,0:T(8,128)(2,1)} %param.7) | copy-start | bytes 4718596
  7.2 93.2 %all-gather.5.cloned.1.call-start = ((), (), s32[]{:S(2)}) async-start(), calls=%async_computation.6 | async-start | bytes 5308416 | tf_op jit(solution)/shard_map/all_gather | solution.py:64
  18.0 130.3 %all-gather.7.cloned.1.call-start = ((), (), s32[]{:S(2)}) async-start(), calls=%async_computation.7 | async-start | bytes 2359296 | tf_op jit(solution)/shard_map/all_gather | solution.py:65
  24.6 173.7 %all-gather.9.cloned.1.call-start = ((), (), s32[]{:S(2)}) async-start(), calls=%async_computation.8 | async-start | bytes 2359296 | tf_op jit(solution)/shard_map/all_gather | solution.py:66
  32.7 273.2 %reduce-scatter.15.cloned.1.call-start = ((), (), s32[]{:S(2)}) async-start(), calls=%async_computation.13 | async-start | bytes 4718592 | tf_op jit(solution)/shard_map/reduce_scatter | solution.py:192
  51.7 4.1 copy-start.122
  51.7 5.5 copy-start.125
  151.6 4.0 copy-start.113
  201.9 7.8 %copy-start.4 = (f32[512,512]{0,1:T(8,128)}, f32[512,512]{0,1:T(8,128)S(1)}, u32[]{:S(2)}) copy-start(f32[512,512]{0,1:T(8,128)S(1)} %fusion.200) | copy-start | bytes 3145732
  203.3 6.5 copy-start.6
  205.2 4.5 copy-start.8
  205.6 4.2 copy-start.62
  207.9 4.6 copy-start.66
  219.4 178.1 %reduce-scatter.11.cloned.1.call-start = ((), (), s32[]{:S(2)}) async-start(), calls=%async_computation.11 | async-start | bytes 4718592 | tf_op jit(solution)/shard_map/reduce_scatter | solution.py:191
  219.4 7.6 %copy-start.22 = (bf16[1536,512]{0,1:T(8,128)(2,1)S(1)}, bf16[1536,512]{0,1:T(8,128)(2,1)}, u32[]{:S(2)}) copy-start(bf16[1536,512]{0,1:T(8,128)(2,1)} %fusion.155) | copy-start | bytes 4718596
  219.4 9.0 %copy-start.124 = (bf16[2048,512]{1,0:T(8,128)(2,1)S(1)}, bf16[2048,512]{1,0:T(8,128)(2,1)}, u32[]{:S(2)}) copy-start(bf16[2048,512]{1,0:T(8,128)(2,1)} %all-gather.9.cloned.1.call-done) | copy-start | bytes 6291460
  247.5 317.1 %reduce-scatter.7.cloned.1.call-start = ((), (), s32[]{:S(2)}) async-start(), calls=%async_computation.9 | async-start | bytes 10616832 | tf_op jit(solution)/shard_map/reduce_scatter | solution.py:190
  261.5 7.2 %copy-start.55 = (bf16[1504,512]{0,1:T(8,128)(2,1)S(1)}, bf16[1504,512]{0,1:T(8,128)(2,1)}, u32[]{:S(2)}) copy-start(bf16[1504,512]{0,1:T(8,128)(2,1)} %get-tuple-element.55) | copy-start | bytes 4620292
  261.5 7.2 %copy-start.70 = (bf16[32,512]{0,1:T(8,128)(2,1)S(1)}, bf16[32,512]{0,1:T(8,128)(2,1)}, u32[]{:S(2)}) copy-start(bf16[32,512]{0,1:T(8,128)(2,1)} %get-tuple-element.57) | copy-start | bytes 98308
  261.5 7.2 %copy-start.120 = (bf16[1536]{0:T(1024)(128)(2,1)S(1)}, bf16[1536]{0:T(1024)(128)(2,1)}, u32[]{:S(2)}) copy-start(bf16[1536]{0:T(1024)(128)(2,1)} %get-tuple-element.93) | copy-start | bytes 9220
  287.2 18.8 %copy-start.80 = (f32[1536]{0:T(1024)S(1)}, f32[1536]{0:T(1024)}, u32[]{:S(2)}) copy-start(f32[1536]{0:T(1024)} %get-tuple-element.94) | copy-start | bytes 18436
  287.2 22.5 %copy-start.79 = (f32[1536]{0:T(1024)S(1)}, f32[1536]{0:T(1024)}, u32[]{:S(2)}) copy-start(f32[1536]{0:T(1024)} %get-tuple-element.92) | copy-start | bytes 18436
  287.2 355.7 %reduce-scatter.17.cloned.1.call-start = ((), (), s32[]{:S(2)}) async-start(), calls=%async_computation.14 | async-start | bytes 655360 | tf_op jit(solution)/shard_map/reduce_scatter | solution.py:198
  306.0 337.0 %reduce-scatter.13.cloned.1.call-start = ((), (), s32[]{:S(2)}) async-start(), calls=%async_computation.12 | async-start | bytes 655360 | tf_op jit(solution)/shard_map/reduce_scatter | solution.py:197
  313.4 84.4 %copy-start.77 = (f32[1536]{0:T(1024)S(1)}, f32[1536]{0:T(1024)}, u32[]{:S(2)}) copy-start(f32[1536]{0:T(1024)} %get-tuple-element.88) | copy-start | bytes 18436
  317.3 84.3 %copy-start.76 = (f32[1536]{0:T(1024)S(1)}, f32[1536]{0:T(1024)}, u32[]{:S(2)}) copy-start(f32[1536]{0:T(1024)} %get-tuple-element.86) | copy-start | bytes 18436
  397.6 245.4 %reduce-scatter.9.cloned.1.call-start = ((), (), s32[]{:S(2)}) async-start(), calls=%async_computation.10 | async-start | bytes 1474560 | tf_op jit(solution)/shard_map/reduce_scatter | solution.py:196
  405.2 159.4 %copy-start.74 = (f32[1536]{0:T(1024)S(1)}, f32[1536]{0:T(1024)}, u32[]{:S(2)}) copy-start(f32[1536]{0:T(1024)} %get-tuple-element.82) | copy-start | bytes 18436
  566.9 13.5 %copy-start.20 = (f32[1536,512]{0,1:T(8,128)}, f32[1536,512]{0,1:T(8,128)S(1)}, u32[]{:S(2)}) copy-start(f32[1536,512]{0,1:T(8,128)S(1)} %convolution_multiply_fusion.1) | copy-start | bytes 9437188
  566.9 4.2 copy-start.15
  576.2 4.0 copy-start.19
  576.2 4.3 copy-start.73
  (108 other events, 247.1 us)
Sparse Core Ops, SparseCore 0:
  18.1 80.4 all-gather.4
  100.8 47.5 all-gather.6
  150.5 47.7 all-gather.8
  219.5 86.3 reduce-scatter.14
  309.8 87.6 reduce-scatter.10
  401.0 163.5 reduce-scatter.6
  567.7 20.7 reduce-scatter.16
  591.7 21.6 reduce-scatter.12
  616.5 25.7 reduce-scatter.8
where the time goes:
time: 656 us; the launch traced here: 650 us
  waiting for transfers between devices  315 us (48%)
  matrix products  123 us (19%)
  blocking collectives  104 us (16%)
  local copies, waits for them, and re-layouts  60.5 us (9%)
  other arithmetic  29.1 us (4%)
  between operations  17.6 us (3%)
    reduce_scatter x1, waiting for transfers between devices, shards(): lax.psum_scatter(convolution_weight_gradient, 'wide', scatter_dimension=1...  156 us
    reduce_scatter x1, waiting for transfers between devices, shards(): lax.psum_scatter(grad_in, 'wide', scatter_dimension=0, tiled=True)  80.3 us
    unnamed x3, blocking collectives  47.6 us
    dot_general x9, matrix products, shards(): jnp.einsum('ro,io->ri', convolution_reduced, conv_full[index_of_tap], pre...  39.2 us
    all_gather x1, waiting for transfers between devices, fetch_forward(): lax.all_gather(narrow_set[2], 'wide', axis=0, tiled=True)  36.4 us
    all_gather x1, blocking collectives, fetch_forward(): lax.all_gather(narrow_set[3], 'wide', axis=0, tiled=True)  31.2 us
    unnamed x270, local copies, waits for them, and re-layouts  28.5 us
    all_gather x1, waiting for transfers between devices, fetch_forward(): lax.all_gather(narrow_set[1], 'wide', axis=0, tiled=True)  26.8 us
  transfers between devices with their start and end apart: 9, of which 5 were waited for; matrix products, arithmetic and copies ran while one was open for 27% of the time, Pallas kernels for 0%

commit v1 on v0

--- a/solution.py
+++ b/solution.py
@@ -1,16 +1,17 @@
+import functools
+
 import jax
 import jax.numpy as jnp
 from jax import lax
+from jax.experimental import pallas as pl
+from jax.experimental.pallas import tpu as pltpu
 from jax.sharding import PartitionSpec as P
 
 D = 512
 FF = 2048
 KERNEL_TAPS = 9
 DILATION_STEP = 8
-
-
 EPSILON = 1e-05
-
 
 def layer_norm(values, norm_gain, norm_shift):
     centre = values - jnp.mean(values, axis=-1, keepdims=True)
@@ -54,21 +55,6 @@
 
 
 def fetch_forward(conv_weight, feedforward_input_weight, ffn_out, small_params):
-    narrow_set = (
-        lax.all_gather(conv_weight, "narrow", axis=2, tiled=True),
-        lax.all_gather(feedforward_input_weight, "narrow", axis=1, tiled=True),
-        lax.all_gather(ffn_out, "narrow", axis=1, tiled=True),
-        lax.all_gather(small_params, "narrow", axis=0, tiled=True),
-    )
-    return (
-        lax.all_gather(narrow_set[0], "wide", axis=1, tiled=True),
-        lax.all_gather(narrow_set[1], "wide", axis=0, tiled=True),
-        lax.all_gather(narrow_set[2], "wide", axis=0, tiled=True),
-        lax.all_gather(narrow_set[3], "wide", axis=0, tiled=True),
-    )
-
-
-def fetch_backward(conv_weight, feedforward_input_weight, ffn_out, small_params):
     narrow_set = (
         lax.all_gather(conv_weight, "narrow", axis=2, tiled=True),
         lax.all_gather(feedforward_input_weight, "narrow", axis=1, tiled=True),
@@ -123,9 +109,6 @@
     upstream = cotangent.astype(jnp.float32) * live_rows[:, None]
     d_outer, d_outer_bias, d_gain_two, d_shift_two = pull_two(upstream)
     outer_low = d_outer.astype(jnp.bfloat16)
-    weights = fetch_backward(conv_weight, feedforward_input_weight, ffn_out, small_params)
-    conv_full, inner_full, outer_full = (weights[0], weights[1], weights[2])
-    pieces = split_params(weights[3].astype(jnp.float32))
     grad_in = jnp.zeros((D, FF), jnp.float32)
     grad_out = jnp.zeros((FF, D), jnp.float32)
     inner_bias_grad = jnp.zeros((FF,), jnp.float32)
@@ -201,10 +184,706 @@
     owned_flat = owned[3]
     return (block_out, grad_tokens, owned[0], owned[1], owned[2], owned_flat)
 
+MESH = pl.DeviceIdType.MESH
+BF = jnp.bfloat16
+F32 = jnp.float32
+BLOCK = 256
+REACH = KERNEL_TAPS // 2 * DILATION_STEP
+STEP_ROWS = 512
+PARAM_ROWS = 48
+GRAD_ROWS = 40
+VMEM_LIMIT = 63 << 20
+GELU_A = 0.7978845608028654
+GELU_B = 0.044715
+TAP_PIECES = ((0, 1), (1, 3), (3, 6), (6, 9))
+GRAD_TAP_PIECES = ((0, 3), (3, 6), (6, 9))
+
+
+class Links:
+    def __init__(self, sizes, send_sems, recv_sems):
+        self.Z, self.X, self.Y = sizes
+        wide, narrow = lax.axis_index("wide"), lax.axis_index("narrow")
+        self.z, self.x = wide // self.X, wide % self.X
+        self.y, self.c = narrow // 2, narrow % 2
+        self.send_sems, self.recv_sems = send_sems, recv_sems
+        self.used = 0
+        self.copies = []
+
+    def device(self, axis, step):
+        z, x, y, c = self.z, self.x, self.y, self.c
+        if axis == "z":
+            z = lax.rem(z + step, self.Z)
+        elif axis == "x":
+            x = lax.rem(x + step, self.X)
+        elif axis == "y":
+            y = lax.rem(y + step, self.Y)
+        else:
+            c = 1 - c
+        return (z * self.X + x, y * 2 + c)
+
+    def steps(self, axis):
+        return range(1, {"z": self.Z, "x": self.X, "y": self.Y, "c": 2}[axis])
+
+    def send(self, source, target, axis, step=1):
+        index = self.used
+        self.used += 1
+        copy = pltpu.make_async_remote_copy(
+            src_ref=source,
+            dst_ref=target,
+            send_sem=self.send_sems.at[index],
+            recv_sem=self.recv_sems.at[index],
+            device_id=self.device(axis, step),
+            device_id_type=MESH,
+        )
+        copy.start()
+        self.copies.append(copy)
+        return copy
+
+    def barrier(self):
+        semaphore = pltpu.get_barrier_semaphore()
+        partners = [self.device(axis, s) for axis in "zxyc" for s in self.steps(axis)]
+        for partner in partners:
+            pl.semaphore_signal(semaphore, inc=1, device_id=partner, device_id_type=MESH)
+        pl.semaphore_wait(semaphore, len(partners))
+
+    def finish(self):
+        for copy in self.copies:
+            copy.wait_send()
+
+
+class Gather:
+    def __init__(self, links, shard, whole, first, last):
+        self.links, self.shard, self.whole = links, shard, whole
+        self.taps = pl.ds(first, last - first)
+        half = whole.shape[5] // 2
+        self.low, self.high = pl.ds(0, half), pl.ds(half, half)
+
+    def along_z(self):
+        k = self.links
+        target = self.whole.at[self.taps, k.y, k.c, k.z, k.x]
+        self.waits = [k.send(self.shard.at[self.taps], target, "z", s) for s in k.steps("z")]
+
+    def first(self, own=None):
+        k = self.links
+        for copy in self.waits:
+            copy.wait_recv()
+        if own is not None:
+            own.wait()
+        low = self.whole.at[self.taps, k.y, k.c, :, k.x, self.low]
+        high = self.whole.at[self.taps, k.y, k.c, :, k.x, self.high]
+        self.lows = [k.send(low, low, "x", s) for s in k.steps("x")]
+        self.highs = [k.send(high, high, "y", s) for s in k.steps("y")]
+
+    def second(self):
+        k = self.links
+        for copy in self.lows:
+            copy.wait_recv()
+        low = self.whole.at[self.taps, k.y, k.c, :, :, self.low]
+        self.waits = [k.send(low, low, "y", s) for s in k.steps("y")]
+        for copy in self.highs:
+            copy.wait_recv()
+        high = self.whole.at[self.taps, :, k.c, :, k.x, self.high]
+        self.waits += [k.send(high, high, "x", s) for s in k.steps("x")]
+
+    def to_core(self):
+        k = self.links
+        for copy in self.waits:
+            copy.wait_recv()
+        own = self.whole.at[self.taps, :, k.c]
+        self.last = k.send(own, own, "c")
+
+    def arrive(self):
+        self.last.wait_recv()
+
+
+class Scatter:
+    def __init__(self, links, buffers, half, first, last, finish):
+        self.links, self.half, self.finish = links, half, finish
+        self.taps = pl.ds(first, last - first)
+        self.partial, self.pair, self.one, self.two, self.three = buffers
+
+    def to_core(self):
+        k, h, t = self.links, self.half, self.taps
+        self.wait = [k.send(self.partial.at[1 - k.c, h, t], self.pair.at[h, t], "c")]
+
+    def first(self):
+        k, h, t, pair = self.links, self.half, self.taps, self.pair
+        for copy in self.wait:
+            copy.wait_recv()
+        pair[h, t] = pair[h, t] + self.partial[k.c, h, t]
+        if h == 0:
+            self.wait = [
+                k.send(pair.at[h, t, lax.rem(k.y + s, k.Y)], self.one[h].at[s - 1, t], "y", s)
+                for s in k.steps("y")
+            ]
+        else:
+            self.wait = [
+                k.send(pair.at[h, t, :, :, lax.rem(k.x + s, k.X)], self.one[h].at[s - 1, t], "x", s)
+                for s in k.steps("x")
+            ]
+
+    def second(self):
+        k, h, t, pair, one = self.links, self.half, self.taps, self.pair, self.one[self.half]
+        for copy in self.wait:
+            copy.wait_recv()
+        if h == 0:
+            for s in k.steps("y"):
+                pair[h, t, k.y] = pair[h, t, k.y] + one[s - 1, t]
+            self.wait = [
+                k.send(pair.at[h, t, k.y, :, lax.rem(k.x + s, k.X)], self.two[h].at[s - 1, t], "x", s)
+                for s in k.steps("x")
+            ]
+        else:
+            for s in k.steps("x"):
+                pair[h, t, :, :, k.x] = pair[h, t, :, :, k.x] + one[s - 1, t]
+            self.wait = [
+                k.send(pair.at[h, t, lax.rem(k.y + s, k.Y), :, k.x], self.two[h].at[s - 1, t], "y", s)
+                for s in k.steps("y")
+            ]
+
+    def along_z(self):
+        k, h, t, pair, two = self.links, self.half, self.taps, self.pair, self.two[self.half]
+        for copy in self.wait:
+            copy.wait_recv()
+        for s in k.steps("x" if h == 0 else "y"):
+            pair[h, t, k.y, :, k.x] = pair[h, t, k.y, :, k.x] + two[s - 1, t]
+        self.wait = [
+            k.send(pair.at[h, t, k.y, lax.rem(k.z + s, k.Z), k.x], self.three.at[s - 1, h, t], "z", s)
+            for s in k.steps("z")
+        ]
+
+    def arrive(self):
+        k, h, t = self.links, self.half, self.taps
+        for copy in self.wait:
+            copy.wait_recv()
+        total = self.pair[h, t, k.y, k.z, k.x].astype(F32)
+        for s in k.steps("z"):
+            total = total + self.three[s - 1, h, t].astype(F32)
+        self.finish(total, h, t)
+
+
+def gelu_pair(value):
+    square = value * value
+    bend = jnp.tanh(value * (GELU_A + (GELU_A * GELU_B) * square))
+    share = 0.5 + 0.5 * bend
+    slope = share + (0.5 * value) * ((1.0 - bend * bend) * (GELU_A + (3 * GELU_A * GELU_B) * square))
+    return value * share, slope
+
+
+def normalize(value):
+    centre = value - jnp.mean(value, axis=-1, keepdims=True)
+    factor = lax.rsqrt(jnp.mean(centre * centre, axis=-1, keepdims=True) + EPSILON)
+    return centre * factor, factor
+
+
+def normalize_back(grad, hat, factor):
+    return factor * (
+        grad
+        - jnp.mean(grad, axis=-1, keepdims=True)
+        - hat * jnp.mean(grad * hat, axis=-1, keepdims=True)
+    )
+
+
+def side_by_side(whole, tap):
+    lanes = whole.shape[-1]
+    return jnp.concatenate(
+        [whole[tap, y, c].reshape(-1, lanes) for y in range(whole.shape[1]) for c in range(2)], axis=1
+    )
+
+
+def dot(left, right, over=((1,), (0,))):
+    return lax.dot_general(left, right, (over, ((), ())), preferred_element_type=F32)
+
+
+OVER_ROWS = ((0,), (0,))
+OVER_LANES = ((1,), (1,))
+
+
+def kernel(
+    sizes, lengths, params_in, tokens, cotangent, conv_in, inner_in, outer_in,
+    block_out, grad_tokens, conv_out, inner_out, outer_out, params_out,
+    conv_w, inner_w, outer_w, params_got, params_sum,
+    rows_buf, cot_buf, padded, padded_by8, padded_back, stage, conv_sum, resid, resid_low, active, slope, outer_low,
+    conv_partial, inner_partial, outer_partial,
+    conv_pair, inner_pair, outer_pair,
+    conv_one_a, conv_one_b, inner_one_a, inner_one_b, outer_one_a, outer_one_b,
+    conv_two_a, conv_two_b, inner_two_a, inner_two_b, outer_two_a, outer_two_b,
+    conv_three, inner_three, outer_three,
+    grads, grads_got,
+    send_sems, recv_sems, local_sems,
+):
+    k = Links(sizes, send_sems, recv_sems)
+    Z, X, Y = sizes
+    row_count = tokens.shape[0]
+    blocks = row_count // BLOCK
+    steps = row_count // STEP_ROWS
+    per_step = STEP_ROWS // BLOCK
+    mine = k.y, k.c, k.z, k.x
+
+    def local(index, source, target):
+        copy = pltpu.make_async_copy(source, target, local_sems.at[index])
+        copy.start()
+        return copy
+
+    rows_in = local(0, tokens, rows_buf)
+    own = [
+        local(1 + i, shard, whole.at[:, k.y, k.c, k.z, k.x])
+        for i, (shard, whole) in enumerate(((conv_in, conv_w), (inner_in, inner_w), (outer_in, outer_w)))
+    ]
+    cot_in = local(4, cotangent, cot_buf)
+    k.barrier()
+
+    pieces = [Gather(k, conv_in, conv_w, first, last) for first, last in TAP_PIECES]
+    pieces += [Gather(k, inner_in, inner_w, 0, 1), Gather(k, outer_in, outer_w, 0, 1)]
+    own_of = {0: own[0], len(TAP_PIECES): own[1], len(TAP_PIECES) + 1: own[2]}
+    count = len(pieces)
+
+    bounds = []
+    total = 0
+    for slot in range(lengths.shape[1]):
+        total = total + lengths[0, slot]
+        bounds.append(total)
+
+    def window(block):
+        number = 0
+        for bound in bounds:
+            number = number + jnp.where(block * BLOCK >= bound, 1, 0)
+        return number
+
+    def live(block):
+        return jnp.where(block * BLOCK < total, 1.0, 0.0).astype(F32)
+
+    def joined(block):
+        return jnp.where(window(block) == window(block + 1), 1.0, 0.0).astype(F32) * live(block)
+
+    def pad(source, target, target_by8):
+        for b in range(blocks):
+            at = b * BLOCK
+            if b > 0:
+                stage[0:REACH] = source[at - REACH : at].astype(F32) * joined(b - 1)
+            else:
+                stage[0:REACH] = jnp.zeros((REACH, D), F32)
+            stage[REACH : REACH + BLOCK] = source[at : at + BLOCK].astype(F32) * live(b)
+            if b < blocks - 1:
+                stage[REACH + BLOCK :] = source[at + BLOCK : at + BLOCK + REACH].astype(F32) * joined(b)
+            else:
+                stage[REACH + BLOCK :] = jnp.zeros((REACH, D), F32)
+            target[b] = stage[...].astype(BF)
+            target_by8[b] = stage[8 : BLOCK + 2 * REACH - 8].astype(BF)
+
+    def window_rows(source, source_by8, block, place):
+        if place % 2 == 0:
+            return source[block, pl.ds(8 * place, BLOCK), :]
+        return source_by8[block, pl.ds(8 * (place - 1), BLOCK), :]
+
+    def step_rows(source, source_by8, step, place):
+        return jnp.concatenate(
+            [window_rows(source, source_by8, step * per_step + j, place) for j in range(per_step)], axis=0
+        )
+
+    def all_rows(source, source_by8, place):
+        return jnp.concatenate([window_rows(source, source_by8, b, place) for b in range(blocks)], axis=0)
+
+    def at_step(step):
+        return pl.ds(pl.multiple_of(step * STEP_ROWS, STEP_ROWS), STEP_ROWS)
+
+    def live_rows(value, step):
+        return jnp.concatenate(
+            [value[j * BLOCK : (j + 1) * BLOCK] * live(step * per_step + j) for j in range(per_step)], axis=0
+        )
+
+    def param(first, width):
+        return jnp.concatenate(
+            [params_sum[4, pl.ds((first + i) // 128, 1), :].astype(F32) for i in range(0, width, 128)], axis=1
+        )
+
+    def add_grad(first, value):
+        summed = jnp.sum(value, axis=0, keepdims=True)
+        for i in range(0, summed.shape[1], 128):
+            row = (first + i) // 128
+            grads[0, row : row + 1, :] = grads[0, row : row + 1, :] + summed[:, i : i + 128]
+
+    CONV_BIAS, GAIN_ONE, SHIFT_ONE, INNER_BIAS = 0, D, 2 * D, 3 * D
+    OUTER_BIAS, GAIN_TWO, SHIFT_TWO = 3 * D + FF, 4 * D + FF, 5 * D + FF
+
+    slot_at = {"z": 0, "x": Z - 1, "y": Z + X - 2, "c": Z + X + Y - 3}
+
+    def share(source, got, axis):
+        return [k.send(source, got.at[slot_at[axis] + s - 1], axis, s) for s in k.steps(axis)]
+
+    def take(copies, source, got, axis):
+        for copy in copies:
+            copy.wait_recv()
+        value = source[...]
+        for s in k.steps(axis):
+            value = value + got[slot_at[axis] + s - 1]
+        return value
+
+    def sum_on(copies, held, got, axes, stage_index):
+        held[stage_index + 1] = take(copies, held.at[stage_index], got, axes[stage_index])
+        if stage_index + 1 < len(axes):
+            return share(held.at[stage_index + 1], got, axes[stage_index + 1])
+        return []
+
+    def conv_piece(piece):
+        first, last = TAP_PIECES[piece]
+
+        @pl.loop(0, steps)
+        def _(step):
+            value = None
+            for tap in range(first, last):
+                term = dot(step_rows(padded, padded_by8, step, tap), side_by_side(conv_w, tap))
+                value = term if value is None else value + term
+            if piece > 0:
+                value = value + conv_sum[at_step(step), :]
+            if piece == len(TAP_PIECES) - 1:
+                value = value + param(CONV_BIAS, D)
+            conv_sum[at_step(step), :] = value
+            if piece == len(TAP_PIECES) - 1:
+                start = step_rows(padded, padded_by8, step, REACH // 8).astype(F32)
+                hat, _ = normalize(gelu_pair(value)[0])
+                value = start + hat * param(GAIN_ONE, D) + param(SHIFT_ONE, D)
+                resid[at_step(step), :] = value
+                resid_low[at_step(step), :] = value.astype(BF)
+
+    width = inner_w.shape[-1]
+
+    def inner_step(step):
+        low = resid_low[at_step(step), :]
+        for y in range(Y):
+            for c in range(2):
+                first = (y * 2 + c) * width
+                value = dot(low, inner_w[0, y, c].reshape(D, width)) + param(INNER_BIAS + first, width)
+                bent, tilt = gelu_pair(value)
+                active[at_step(step), first : first + width] = bent.astype(BF)
+                slope[at_step(step), first : first + width] = tilt.astype(BF)
+
+    def outer_step(step):
+        value = dot(active[at_step(step), :], side_by_side(outer_w, 0)) + param(OUTER_BIAS, D)
+        hat, factor = normalize(value)
+        gain = param(GAIN_TWO, D)
+        result = resid[at_step(step), :] + hat * gain + param(SHIFT_TWO, D)
+        rows_buf[at_step(step), :] = live_rows(result, step).astype(BF)
+        upstream = live_rows(cot_buf[at_step(step), :].astype(F32), step)
+        back = normalize_back(upstream * gain, hat, factor)
+        outer_low[at_step(step), :] = back.astype(BF)
+        add_grad(OUTER_BIAS, back)
+        add_grad(GAIN_TWO, upstream * hat)
+        add_grad(SHIFT_TWO, upstream)
+
+    outer_rows = outer_w.shape[5]
+
+    def outer_grad(half):
+        size = outer_rows // 2
+        left = jnp.concatenate(
+            [active[:, i * outer_rows + half * size : i * outer_rows + (half + 1) * size] for i in range(Z * X)],
+            axis=1,
+        )
+        value = dot(left, outer_low[...], OVER_ROWS).astype(BF)
+        for y in range(Y):
+            for c in range(2):
+                first = (y * 2 + c) * 128
+                outer_partial[c, half, 0, y] = value[:, first : first + 128].reshape(Z, X, size, 128)
+
+    def hidden_step(step):
+        low = outer_low[at_step(step), :]
+        for group in range(Y * 2):
+            first = group * width
+            right = jnp.concatenate(
+                [outer_w[0, y, c, group].reshape(width, 128) for y in range(Y) for c in range(2)], axis=1
+            )
+            value = dot(low, right, OVER_LANES)
+            value = value * slope[at_step(step), first : first + width].astype(F32)
+            add_grad(INNER_BIAS + first, value)
+            slope[at_step(step), first : first + width] = value.astype(BF)
+
+    def inner_grad(half):
+        size = width // 2
+        right = jnp.concatenate(
+            [slope[:, g * width + half * size : g * width + (half + 1) * size] for g in range(Y * 2)], axis=1
+        )
+        value = dot(resid_low[...], right, OVER_ROWS).astype(BF)
+        for y in range(Y):
+            for c in range(2):
+                first = (y * 2 + c) * size
+                inner_partial[c, half, 0, y] = value[:, first : first + size].reshape(Z, X, D // (Z * X), size)
+
+    def resid_step(step):
+        value = live_rows(cot_buf[at_step(step), :].astype(F32), step)
+        for y in range(Y):
+            for c in range(2):
+                first = (y * 2 + c) * width
+                value = value + dot(
+                    slope[at_step(step), first : first + width], inner_w[0, y, c].reshape(D, width), OVER_LANES
+                )
+        resid[at_step(step), :] = value
+        bent, tilt = gelu_pair(conv_sum[at_step(step), :])
+        hat, factor = normalize(bent)
+        add_grad(GAIN_ONE, value * hat)
+        add_grad(SHIFT_ONE, value)
+        back = normalize_back(value * param(GAIN_ONE, D), hat, factor) * tilt
+        add_grad(CONV_BIAS, back)
+        conv_sum[at_step(step), :] = back
+
+    conv_rows = conv_w.shape[5]
+
+    def conv_grad(first, last):
+        left = all_rows(padded, None, REACH // 8)
+        for tap in range(first, last):
+            right = all_rows(padded_back, padded_by8, KERNEL_TAPS - 1 - tap)
+            value = dot(left, right, OVER_ROWS).astype(BF)
+            for y in range(Y):
+                for c in range(2):
+                    at = (y * 2 + c) * 128
+                    part = value[:, at : at + 128].reshape(Z, X, conv_rows, 128)
+                    for half in range(2):
+                        size = conv_rows // 2
+                        conv_partial[c, half, tap, y] = part[:, :, half * size : (half + 1) * size]
+
+    def token_step(step):
+        value = resid[at_step(step), :]
+        for tap in range(KERNEL_TAPS):
+            value = value + dot(
+                step_rows(padded_back, padded_by8, step, KERNEL_TAPS - 1 - tap),
+                side_by_side(conv_w, tap),
+                OVER_LANES,
+            )
+        resid[at_step(step), :] = live_rows(value, step)
+
+    def conv_finish(value, half, taps):
+        size = conv_rows // 2
+        conv_out[taps, pl.ds(half * size, size), :] = value
+
+    def inner_finish(value, half, taps):
+        size = width // 2
+        inner_out[:, half * size : (half + 1) * size] = value[0]
+
+    def outer_finish(value, half, taps):
+        size = outer_rows // 2
+        outer_out[half * size : (half + 1) * size, :] = value[0]
+
+    params_sum[0] = params_in[...]
+    sharing = share(params_in, params_got, "z")
+    pieces[0].along_z()
+    pieces[1].along_z()
+    rows_in.wait()
+    grads[0] = jnp.zeros((GRAD_ROWS, 128), F32)
+    pad(rows_buf, padded, padded_by8)
+    turn = ["z", "x", "y", "c"]
+    for i in range(count + 3):
+        if 0 < i and i + 1 < count:
+            pieces[i + 1].along_z()
+        if i < count:
+            pieces[i].first(own_of.get(i))
+        if 0 <= i - 1 < count:
+            pieces[i - 1].second()
+        if i < 4:
+            sharing = sum_on(sharing, params_sum, params_got, turn, i)
+        if 0 <= i - 2 < count:
+            pieces[i - 2].to_core()
+        if 0 <= i - 3 < len(TAP_PIECES):
+            pieces[i - 3].arrive()
+            conv_piece(i - 3)
+    pieces[count - 2].arrive()
+    pl.loop(0, steps)(inner_step)
+    pieces[count - 1].arrive()
+    cot_in.wait()
+    pl.loop(0, steps)(outer_step)
+    block_copy = local(0, rows_buf, block_out)
+
+    outer_buffers = (outer_partial, outer_pair, (outer_one_a, outer_one_b), (outer_two_a, outer_two_b), outer_three)
+    inner_buffers = (inner_partial, inner_pair, (inner_one_a, inner_one_b), (inner_two_a, inner_two_b), inner_three)
+    conv_buffers = (conv_partial, conv_pair, (conv_one_a, conv_one_b), (conv_two_a, conv_two_b), conv_three)
+    outers = [Scatter(k, outer_buffers, half, 0, 1, outer_finish) for half in range(2)]
+    inners = [Scatter(k, inner_buffers, half, 0, 1, inner_finish) for half in range(2)]
+    convs = [
+        Scatter(k, conv_buffers, half, first, last, conv_finish)
+        for first, last in GRAD_TAP_PIECES
+        for half in range(2)
+    ]
+    outer_grad(0)
+    outers[0].to_core()
+    outer_grad(1)
+    outers[1].to_core()
+    outers[0].first()
+    hidden_step(0)
+    outers[1].first()
+    hidden_step(1)
+    outers[0].second()
+    hidden_step(2)
+    outers[1].second()
+    inner_grad(0)
+    inners[0].to_core()
+    outers[0].along_z()
+    inner_grad(1)
+    inners[1].to_core()
+    inners[0].first()
+    outers[1].along_z()
+    resid_step(0)
+    inners[1].first()
+    resid_step(1)
+    inners[0].second()
+    outers[0].arrive()
+    resid_step(2)
+    inners[1].second()
+    outers[1].arrive()
+    back_turn = ["c", "x", "y", "z"]
+    sharing = share(grads.at[0], grads_got, "c")
+    pad(conv_sum, padded_back, padded_by8)
+    conv_grad(0, 3)
+    convs[0].to_core()
+    convs[1].to_core()
+    inners[0].along_z()
+    inners[1].along_z()
+    sharing = sum_on(sharing, grads, grads_got, back_turn, 0)
+    conv_grad(3, 6)
+    sharing = sum_on(sharing, grads, grads_got, back_turn, 1)
+    convs[0].first()
+    convs[1].first()
+    convs[2].to_core()
+    convs[3].to_core()
+    conv_grad(6, 9)
+    sharing = sum_on(sharing, grads, grads_got, back_turn, 2)
+    convs[2].first()
+    convs[3].first()
+    convs[4].to_core()
+    convs[5].to_core()
+    convs[0].second()
+    convs[1].second()
+    inners[0].arrive()
+    inners[1].arrive()
+    token_step(0)
+    params_out[...] = take(sharing, grads.at[3], grads_got, "z")
+    convs[4].first()
+    convs[5].first()
+    convs[2].second()
+    convs[3].second()
+    convs[0].along_z()
+    convs[1].along_z()
+    token_step(1)
+    convs[4].second()
+    convs[5].second()
+    convs[2].along_z()
+    convs[3].along_z()
+    token_step(2)
+    token_copy = local(1, resid, grad_tokens)
+    convs[4].along_z()
+    convs[5].along_z()
+    for i in range(4):
+        convs[i].arrive()
+    convs[4].arrive()
+    convs[5].arrive()
+    block_copy.wait()
+    token_copy.wait()
+    k.finish()
+
+
+def run_kernel(sizes, lengths, params, tokens, cotangent, conv_shard, inner_shard, outer_shard):
+    Z, X, Y = sizes
+    taps, conv_rows, lanes = conv_shard.shape
+    inner_rows, width = inner_shard.shape
+    outer_rows = outer_shard.shape[0]
+    rows = tokens.shape[0]
+    blocks = rows // BLOCK
+    inner_shard, outer_shard = inner_shard[None], outer_shard[None]
+
+    def whole(shard):
+        return pltpu.VMEM((shard.shape[0], Y, 2, Z, X) + shard.shape[1:], BF)
+
+    def scatter_buffers(count, r, lane):
+        return (
+            pltpu.VMEM((2, 2, count, Y, Z, X, r, lane), BF),
+            pltpu.VMEM((2, count, Y, Z, X, r, lane), BF),
+            pltpu.VMEM((Y - 1, count, Z, X, r, lane), BF),
+            pltpu.VMEM((X - 1, count, Y, Z, r, lane), BF),
+            pltpu.VMEM((X - 1, count, Z, r, lane), BF),
+            pltpu.VMEM((Y - 1, count, Z, r, lane), BF),
+            pltpu.VMEM((Z - 1, 2, count, r, lane), BF),
+        )
+
+    conv_b = scatter_buffers(taps, conv_rows // 2, lanes)
+    inner_b = scatter_buffers(1, inner_rows, width // 2)
+    outer_b = scatter_buffers(1, outer_rows // 2, lanes)
+    partners = Z - 1 + X - 1 + Y - 1 + 1
+    copies = 16 * (partners + 4)
+    padded = BLOCK + 2 * REACH
+    scratch = [whole(conv_shard), whole(inner_shard), whole(outer_shard)]
+    scratch += [pltpu.VMEM((partners, PARAM_ROWS, 128), BF), pltpu.VMEM((5, PARAM_ROWS, 128), BF)]
+    scratch += [
+        pltpu.VMEM((rows, D), BF),
+        pltpu.VMEM((rows, D), BF),
+        pltpu.VMEM((blocks, padded, D), BF),
+        pltpu.VMEM((blocks, padded - 16, D), BF),
+        pltpu.VMEM((blocks, padded, D), BF),
+        pltpu.VMEM((padded, D), F32),
+        pltpu.VMEM((rows, D), F32),
+        pltpu.VMEM((rows, D), F32),
+        pltpu.VMEM((rows, D), BF),
+        pltpu.VMEM((rows, FF), BF),
+        pltpu.VMEM((rows, FF), BF),
+        pltpu.VMEM((rows, D), BF),
+    ]
+    scratch += [b[0] for b in (conv_b, inner_b, outer_b)]
+    scratch += [b[1] for b in (conv_b, inner_b, outer_b)]
+    scratch += [b[i] for b in (conv_b, inner_b, outer_b) for i in (2, 3)]
+    scratch += [b[i] for b in (conv_b, inner_b, outer_b) for i in (4, 5)]
+    scratch += [b[6] for b in (conv_b, inner_b, outer_b)]
+    scratch += [pltpu.VMEM((5, GRAD_ROWS, 128), F32), pltpu.VMEM((partners, GRAD_ROWS, 128), F32)]
+    scratch += [pltpu.SemaphoreType.DMA((copies,)), pltpu.SemaphoreType.DMA((copies,)), pltpu.SemaphoreType.DMA((8,))]
+    far = pl.BlockSpec(memory_space=pl.ANY)
+    near = pl.BlockSpec(memory_space=pltpu.VMEM)
+    return pl.pallas_call(
+        functools.partial(kernel, sizes),
+        out_shape=[
+            jax.ShapeDtypeStruct((rows, D), BF),
+            jax.ShapeDtypeStruct((rows, D), F32),
+            jax.ShapeDtypeStruct(conv_shard.shape, F32),
+            jax.ShapeDtypeStruct(inner_shard.shape[1:], F32),
+            jax.ShapeDtypeStruct(outer_shard.shape[1:], F32),
+            jax.ShapeDtypeStruct((GRAD_ROWS, 128), F32),
+        ],
+        in_specs=[pl.BlockSpec(memory_space=pltpu.SMEM), near] + [far] * 5,
+        out_specs=[far, far, near, near, near, near],
+        scratch_shapes=scratch,
+        compiler_params=pltpu.CompilerParams(
+            collective_id=0, has_side_effects=True, vmem_limit_bytes=VMEM_LIMIT
+        ),
+    )(lengths, params, tokens, cotangent, conv_shard, inner_shard, outer_shard)
+
+
+def fused(
+    sizes, tokens, window_lengths, conv_weight, feedforward_input_weight, ffn_out, small_params, cotangent
+):
+    share = small_params.shape[0]
+    whole = 6 * D + FF
+    device = lax.axis_index("wide") * (sizes[2] * 2) + lax.axis_index("narrow")
+    places = jnp.arange(PARAM_ROWS * 128, dtype=jnp.int32)
+    params = jnp.where(
+        places // share == device, jnp.tile(small_params, PARAM_ROWS * 128 // share + 1)[: PARAM_ROWS * 128], 0
+    ).reshape(PARAM_ROWS, 128)
+    block_out, grad_tokens, conv_grad, inner_grad, outer_grad, params_grad = run_kernel(
+        sizes, window_lengths, params, tokens, cotangent, conv_weight, feedforward_input_weight, ffn_out
+    )
+    own = lax.dynamic_slice(params_grad.reshape(whole), (device * share,), (share,))
+    return (block_out, grad_tokens, conv_grad, inner_grad, outer_grad, own)
+
 
 def solution(mesh):
+    wide, narrow = mesh.shape["wide"], mesh.shape["narrow"]
+    Y = X = narrow // 2
+    sizes = (wide // X, X, Y)
+
+    def step(*arrays):
+        rows = arrays[0].shape[0]
+        inner, outer = arrays[3].shape, arrays[4].shape
+        whole_lanes = all(a.shape[-1] % 256 == 0 or a.shape[-1] == 128 for a in arrays[2:5])
+        fits = rows % STEP_ROWS == 0 and inner[1] == X * outer[0] and whole_lanes
+        if fits and wide % X == 0 and narrow % 2 == 0:
+            return fused(sizes, *arrays)
+        return shards(*arrays)
+
     return jax.shard_map(
-        shards,
+        step,
         mesh=mesh,
         in_specs=(
             P(("wide", "narrow"), None),

time: 656 us -> 147 us (0.22)
  waiting for transfers between devices: 315 us -> 0 us
  Pallas kernels: 0 us -> 137 us
  matrix products: 123 us -> 0 us
  blocking collectives: 104 us -> 0 us
  local copies, waits for them, and re-layouts: 60.5 us -> 8.61 us
  other arithmetic: 29.1 us -> 0.63 us
  between operations: 17.6 us -> 0.66 us
    reduce_scatter x6 -> x0, waiting for transfers between devices: 252 us -> none  [the longest x1 156 us: shards(): lax.psum_scatter(convolution_weight_gradient, 'wide', scatter_dimension=1...]
    pallas_call x0 -> x1, Pallas kernels: none -> 137 us  [run_kernel(): pl.pallas_call(functools.partial(kernel, sizes), out_shape=[jax.ShapeDtyp...]
    dot_general x45 -> x0, matrix products: 123 us -> none  [the longest x9 39.2 us: shards(): jnp.einsum('ro,io->ri', convolution_reduced, conv_full[index_of_tap], pre...]
    all_gather x3 -> x0, waiting for transfers between devices: 63.2 us -> none  [the longest x1 36.4 us: fetch_forward(): lax.all_gather(narrow_set[2], 'wide', axis=0, tiled=True)]
    all_gather x4 -> x0, blocking collectives: 56.5 us -> none  [the longest x1 31.2 us: fetch_forward(): lax.all_gather(narrow_set[3], 'wide', axis=0, tiled=True)]
    unnamed x3 -> x0, blocking collectives: 47.6 us -> none
    slice x35 -> x0, local copies, waits for them, and re-layouts: 32 us -> none  [the longest x8 14.2 us: shards(): jnp.roll(start_rows, -tap_displacement, axis=0)]
    unnamed x270 -> x13, local copies, waits for them, and re-layouts: 28.5 us -> 6.51 us
  transfers between devices with their start and end apart: 9 -> 0, of which waited for: 5 -> 0; matrix products, arithmetic and copies ran while one was open for 27% -> 0% of each run, Pallas kernels for 0% -> 0%
where the time goes in v1:
time: 147 us; the launch traced here: 146 us
  Pallas kernels  137 us (93%)
  local copies, waits for them, and re-layouts  8.61 us (6%)
    pallas_call x1, Pallas kernels, run_kernel(): pl.pallas_call(functools.partial(kernel, sizes), out_shape=[jax.ShapeDtyp...  137 us
    unnamed x13, local copies, waits for them, and re-layouts  6.51 us

profile of v1, /device:TPU:0, one launch (start us, length us, event | category | flops | bytes accessed | tf_op | source)
XLA Modules:
  0.0 146.5 jit_solution(9233857681912653298)
XLA Ops:
  0.6 0.7 tile.4
  1.3 0.1 tile.10
  1.4 0.6 fusion.1.params_in
  2.0 136.6 %shard_map.118 = (bf16[1536,512]{1,0:T(8,128)(2,1)}, f32[1536,512]{1,0:T(8,128)}, f32[9,64,128]{2,1,0:T(8,128)}, f32[64,512]{1,0:T(8,128)}, f32[256,128]{1,0:T(8,128)}, /*index=5*/f32[40,128]{1,0:T(8,128)}) custom-call(s32[1,6]{1,0:T(1,128)} %lengths.1, bf16[48,128]{1,0:T(8,128)(2,1)} %fusion.1.params_in, bf16[1536,512]{1,0:T(8,128)(2,1)} %tokens.1, ...), custom_call_target="tpu_custom_call" | custom-call | tf_op jit(solution)/shard_map/pallas_call | solution.py:835
  138.6 1.3 dynamic_slice.3
  140.0 0.0 copy-start
  140.0 2.8 %copy.18 = bf16[1536,512]{1,0:T(8,128)(2,1)} copy(bf16[1536,512]{1,0:T(8,128)(2,1)} %get-tuple-element.24) | data formatting | bytes 3145728
  142.8 0.0 copy-done
  142.8 0.0 copy-start.1
  142.8 0.0 copy-start.3
  142.8 0.0 copy-start.2
  142.8 1.7 %copy.19 = f32[1536,512]{1,0:T(8,128)} copy(f32[1536,512]{1,0:T(8,128)S(1)} %copy-done) | data formatting | bytes 6291456
  144.5 0.0 copy-done.1
  144.5 0.7 copy.20
  145.2 0.0 copy-done.3
  145.2 0.7 copy.21
  145.8 0.0 copy-done.2
  145.8 0.7 copy.22
Async XLA Ops:
  140.0 2.8 %copy-start = (f32[1536,512]{1,0:T(8,128)S(1)}, f32[1536,512]{1,0:T(8,128)}, u32[]{:S(2)}) copy-start(f32[1536,512]{1,0:T(8,128)} %get-tuple-element.25) | copy-start | bytes 9437188
  142.8 1.7 %copy-start.1 = (f32[9,64,128]{2,1,0:T(8,128)S(1)}, f32[9,64,128]{2,1,0:T(8,128)}, u32[]{:S(2)}) copy-start(f32[9,64,128]{2,1,0:T(8,128)} %get-tuple-element.26) | copy-start | bytes 884740
  142.8 2.4 %copy-start.3 = (f32[64,512]{1,0:T(8,128)S(1)}, f32[64,512]{1,0:T(8,128)}, u32[]{:S(2)}) copy-start(f32[64,512]{1,0:T(8,128)} %get-tuple-element.27) | copy-start | bytes 393220
  142.8 3.0 %copy-start.2 = (f32[256,128]{1,0:T(8,128)S(1)}, f32[256,128]{1,0:T(8,128)}, u32[]{:S(2)}) copy-start(f32[256,128]{1,0:T(8,128)} %get-tuple-element.28) | copy-start | bytes 393220
